TPU v7x, 32 devices: a whole 2x2x4 slice. The times are simulated.
32 devices in a mesh: pipe: 4 (over y, core), space: 8 (over z, x).
Axes of the slice: x: 2, y: 2, z: 4, core: 2. Of those that a mesh axis runs over, the one named last changes fastest.
Arguments:
- activations: bfloat16 [4, 64, 128, 2048], P('pipe', 'space'), may hold values from -6 to 6
- cotangent: bfloat16 [64, 128, 2048], P('space'), may hold values from -6 to 6
- w_first: bfloat16 [4, 2, 8, 256, 256], P('pipe'), may hold values from -0.25 to 0.25
- w_second: bfloat16 [4, 2, 8, 256, 256], P('pipe'), may hold values from -0.25 to 0.25
- b_first: float32 [4, 2, 2048], P('pipe'), may hold values from -1 to 1
Outputs:
- grads: bfloat16 [4, 64, 128, 2048], P('pipe', 'space')
All inputs are finite; a program needn't handle non-finite values.
Results may differ from a plain program's by a relative error of at most 0.028.
Values may be sent and summed in bfloat16 or wider, within the bound.
A program may use at most 64 MiB of HBM per device.

v0:
```python
import math

import jax
import jax.numpy as jnp
from jax import lax
from jax.sharding import PartitionSpec as P

HIGHEST_MODE = lax.Precision.HIGHEST


def from_behind(block, axis, distance):
    devices = range(lax.axis_size(axis))
    route = [(i - distance, i) for i in devices if i - distance in devices]
    return lax.ppermute(block, axis, route)


def gelu_slope(values):
    return (
        0.5 * (1.0 + lax.erf(values * 0.7071067811865476))
        + values * jnp.exp(-0.5 * values * values) * 0.3989422804014327
    )


def width_table(width_count, mode_count):
    position = jnp.arange(width_count, dtype=jnp.int32)[:, None]
    frequency = jnp.arange(mode_count, dtype=jnp.int32)[None, :]
    angles = (position * frequency % width_count).astype(jnp.float32) * (
        2.0 * math.pi / width_count
    )
    norm_scale = 1.0 / math.sqrt(width_count)
    return jnp.stack([jnp.cos(angles) * norm_scale, -jnp.sin(angles) * norm_scale])


def height_tables(height_count):
    position = jnp.arange(height_count, dtype=jnp.int32)
    angles = (position[:, None] * position[None, :] % height_count).astype(jnp.float32) * (
        2.0 * math.pi / height_count
    )
    norm_scale = 1.0 / math.sqrt(height_count)
    return (jnp.cos(angles) * norm_scale, jnp.sin(angles) * norm_scale)


def row_spectrum(field_values, w_table, doubled):
    spectra = jnp.einsum(
        "hwc,swk->shkc", field_values.astype(jnp.float32), w_table, precision=HIGHEST_MODE
    )
    if doubled:
        factor = jnp.where(jnp.arange(w_table.shape[2]) == 0, 1.0, 2.0).astype(jnp.float32)
        return spectra * factor[None, None, :, None]
    return spectra.astype(jnp.bfloat16)


def column_transform(stacked, cosines, sine_table, forward):
    values = stacked.astype(jnp.float32)
    cos_part = jnp.einsum("kh,shmc->skmc", cosines, values, precision=HIGHEST_MODE)
    sin_part = jnp.einsum("kh,shmc->skmc", sine_table, values, precision=HIGHEST_MODE)
    if forward:
        return jnp.stack([cos_part[0] + sin_part[1], cos_part[1] - sin_part[0]])
    return jnp.stack([cos_part[0] - sin_part[1], cos_part[1] + sin_part[0]])


def first_layer_slope(spectra, layer_one, bias_one):
    block_count, block_size = (layer_one.shape[1], layer_one.shape[2])
    spec_real = spectra[0].reshape(-1, block_count, block_size)
    spec_imag = spectra[1].reshape(-1, block_count, block_size)

    def product(operand, weights):
        return jnp.einsum("tnj,njk->tnk", operand, weights, preferred_element_type=jnp.float32)

    z_real = (
        product(spec_real, layer_one[0])
        - product(spec_imag, layer_one[1])
        + bias_one[0].reshape(block_count, block_size)
    )
    z_imag = (
        product(spec_real, layer_one[1])
        + product(spec_imag, layer_one[0])
        + bias_one[1].reshape(block_count, block_size)
    )
    return jnp.stack([gelu_slope(z_real), gelu_slope(z_imag)]).reshape(
        2, -1, block_count * block_size
    )


def mlp_adjoint(grad_spec, slopes, one_block, two_block):
    block_size = one_block.shape[1]
    grad_real = grad_spec[0].reshape(-1, block_size)
    grad_imag = grad_spec[1].reshape(-1, block_size)

    def adjoint(operand, weights):
        return jnp.dot(operand, weights.T, preferred_element_type=jnp.float32)

    adj_real = adjoint(grad_real, two_block[0]) + adjoint(grad_imag, two_block[1])
    adj_imag = adjoint(grad_imag, two_block[0]) - adjoint(grad_real, two_block[1])
    pre_real = (adj_real * slopes[0]).astype(jnp.bfloat16)
    pre_imag = (adj_imag * slopes[1]).astype(jnp.bfloat16)
    src_real = adjoint(pre_real, one_block[0]) + adjoint(pre_imag, one_block[1])
    src_imag = adjoint(pre_imag, one_block[0]) - adjoint(pre_real, one_block[1])
    return jnp.stack([src_real, src_imag]).astype(jnp.bfloat16).reshape(grad_spec.shape)


def body(activations, cotangent, w_first, w_second, b_first):
    segment_count = lax.axis_size("pipe")
    segment_index = lax.axis_index("pipe")
    own_act = activations[0]
    layer_one = w_first[0]
    layer_two = w_second[0]
    bias_one = b_first[0]
    row_count, width_count, channel_count = own_act.shape
    block_count, block_size = (layer_one.shape[1], layer_one.shape[2])
    height_count = row_count * lax.axis_size("space")
    w_table = width_table(width_count, width_count // 2)
    cosines, sine_table = height_tables(height_count)

    def advance(step_index, state_pair):
        incoming, result = state_pair
        block_index = step_index - (segment_count - 1 - segment_index)
        active = jnp.logical_and(block_index >= 0, block_index < block_count)
        chosen = jnp.clip(block_index, 0, block_count - 1)
        offset = chosen * block_size
        one_block = lax.dynamic_index_in_dim(layer_one, chosen, 1, keepdims=False)
        two_block = lax.dynamic_index_in_dim(layer_two, chosen, 1, keepdims=False)
        act_block = lax.dynamic_slice_in_dim(own_act, offset, block_size, 2)
        spread = lax.all_to_all(
            row_spectrum(act_block, w_table, False),
            "space",
            split_axis=2,
            concat_axis=1,
            tiled=True,
        )
        spectra = column_transform(spread, cosines, sine_table, True).astype(jnp.bfloat16)
        bias_block = lax.dynamic_slice_in_dim(bias_one, offset, block_size, 1)
        slopes = first_layer_slope(spectra, one_block[:, None], bias_block)
        arriving = lax.dynamic_slice_in_dim(cotangent, offset, block_size, 2).astype(jnp.float32)
        grad_in = jnp.where(segment_index == segment_count - 1, arriving, incoming)
        grad_cols = lax.all_to_all(
            row_spectrum(grad_in, w_table, True).astype(jnp.bfloat16),
            "space",
            split_axis=2,
            concat_axis=1,
            tiled=True,
        ).astype(jnp.float32)
        grad_spec = column_transform(grad_cols, cosines, sine_table, True).astype(jnp.bfloat16)
        source = mlp_adjoint(grad_spec, slopes, one_block, two_block)
        back_height = column_transform(source, cosines, sine_table, False).astype(jnp.bfloat16)
        back_rows = lax.all_to_all(back_height, "space", split_axis=1, concat_axis=2, tiled=True)
        spatial = jnp.einsum(
            "shkc,swk->hwc", back_rows.astype(jnp.float32), w_table, precision=HIGHEST_MODE
        )
        carried = spatial + grad_in
        fresh = carried.astype(jnp.bfloat16)
        passed = from_behind(carried.astype(jnp.bfloat16), "pipe", -1).astype(carried.dtype)
        previous = lax.dynamic_slice_in_dim(result, offset, block_size, 2)
        result = lax.dynamic_update_slice_in_dim(
            result, jnp.where(active, fresh, previous), offset, 2
        )
        return (passed, result)

    start_state = jnp.zeros((row_count, width_count, block_size), jnp.float32)
    initial = (start_state, jnp.zeros(own_act.shape, jnp.bfloat16))
    finished = lax.fori_loop(0, block_count + segment_count - 1, advance, initial)
    return finished[1][None]


def solution(mesh):
    in_specs = (
        P("pipe", "space", None, None),
        P("space", None, None),
        P("pipe", None, None, None, None),
        P("pipe", None, None, None, None),
        P("pipe", None, None),
    )
    out_specs = P("pipe", "space", None, None)
    return jax.shard_map(body, mesh=mesh, in_specs=in_specs, out_specs=out_specs, check_vma=False)
```

profile of v0, /device:TPU:15, one launch (start us, length us, event | category | flops | bytes accessed | tf_op | source)
XLA Modules:
  0.0 827.2 jit_solution(12966322802921732137)
XLA Ops:
  2.7 824.5 %while.19 = (s32[]{:T(128)}, f32[8,128,256]{1,2,0:T(8,128)S(1)}, bf16[8,128,2048]{2,1,0:T(8,128)(2,1)}, pred[]{:T(512)}, s32[]{:T(128)}, /*index=5*/bf16[8,128,2...) while((s32[]{:T(128)}, f32[8,128,256]{1,2,0:T(8,128)S(1)}, ...), condition=%wide.region_1.2_spmd.clone.clone, body=%wide.region_0.1_spmd.clone.clone.sunk | while | flops 3230769152 | bytes 75177064 | solution.py:161
  15.3 8.0 all-to-all-done.1
  23.3 6.3 all-to-all-start
  33.9 7.7 all-to-all-done
  54.4 6.3 all-to-all-start.2
  62.2 10.6 %all-to-all-done.2 = bf16[2,64,8,256]{3,2,0,1:T(8,128)(2,1)S(1)} async-done(((bf16[2,64,8,256]{3,2,0,1:T(8,128)(2,1)}), bf16[2,64,8,256]{3,2,0,1:T(8,128)(2,1)S(1)}, u32[]{:S(2)}, u32[]{:S(2)}) %all-to-all-start.2) | async-done | bytes 524320 | tf_op jit(solution)/shard_map/while/body/eval_jaxpr/all_to_all | solution.py:146
  81.6 6.4 all-to-all-start.1
  127.5 6.2 all-to-all-done.2
  135.4 11.2 %collective-permute-start = (bf16[8,128,256]{1,2,0:T(8,128)(2,1)}, bf16[8,128,256]{1,2,0:T(8,128)(2,1)S(1)}, u32[]{:S(2)}, u32[]{:S(2)}) collective-permute-start(bf16[8,128,256]{1,2,0:T(8,128)(2,1)} %get-tuple-element.525), channel_id=1, source_target_pairs={{8,0},{16,8},{24,16},{9,1},{17,9},{25,17},{10,2},{18,10},{26,18},{... | collective-permute-start | bytes 1572872 | tf_op jit(solution)/shard_map/while/body/eval_jaxpr/ppermute | solution.py:14
  173.1 7.9 all-to-all-done
  193.8 6.7 all-to-all-start.2
  201.9 6.2 all-to-all-done.2
  209.7 17.4 %collective-permute-start = (bf16[8,128,256]{1,2,0:T(8,128)(2,1)}, bf16[8,128,256]{1,2,0:T(8,128)(2,1)S(1)}, u32[]{:S(2)}, u32[]{:S(2)}) collective-permute-start(bf16[8,128,256]{1,2,0:T(8,128)(2,1)} %get-tuple-element.525), channel_id=1, source_target_pairs={{8,0},{16,8},{24,16},{9,1},{17,9},{25,17},{10,2},{18,10},{26,18},{... | collective-permute-start | bytes 1572872 | tf_op jit(solution)/shard_map/while/body/eval_jaxpr/ppermute | solution.py:14
  276.1 6.2 all-to-all-done.2
  284.0 12.3 %collective-permute-start = (bf16[8,128,256]{1,2,0:T(8,128)(2,1)}, bf16[8,128,256]{1,2,0:T(8,128)(2,1)S(1)}, u32[]{:S(2)}, u32[]{:S(2)}) collective-permute-start(bf16[8,128,256]{1,2,0:T(8,128)(2,1)} %get-tuple-element.525), channel_id=1, source_target_pairs={{8,0},{16,8},{24,16},{9,1},{17,9},{25,17},{10,2},{18,10},{26,18},{... | collective-permute-start | bytes 1572872 | tf_op jit(solution)/shard_map/while/body/eval_jaxpr/ppermute | solution.py:14
  322.8 7.8 all-to-all-done
  343.4 6.5 all-to-all-start.2
  351.3 6.2 all-to-all-done.2
  359.2 17.5 %collective-permute-start = (bf16[8,128,256]{1,2,0:T(8,128)(2,1)}, bf16[8,128,256]{1,2,0:T(8,128)(2,1)S(1)}, u32[]{:S(2)}, u32[]{:S(2)}) collective-permute-start(bf16[8,128,256]{1,2,0:T(8,128)(2,1)} %get-tuple-element.525), channel_id=1, source_target_pairs={{8,0},{16,8},{24,16},{9,1},{17,9},{25,17},{10,2},{18,10},{26,18},{... | collective-permute-start | bytes 1572872 | tf_op jit(solution)/shard_map/while/body/eval_jaxpr/ppermute | solution.py:14
  425.7 6.2 all-to-all-done.2
  433.6 12.2 %collective-permute-start = (bf16[8,128,256]{1,2,0:T(8,128)(2,1)}, bf16[8,128,256]{1,2,0:T(8,128)(2,1)S(1)}, u32[]{:S(2)}, u32[]{:S(2)}) collective-permute-start(bf16[8,128,256]{1,2,0:T(8,128)(2,1)} %get-tuple-element.525), channel_id=1, source_target_pairs={{8,0},{16,8},{24,16},{9,1},{17,9},{25,17},{10,2},{18,10},{26,18},{... | collective-permute-start | bytes 1572872 | tf_op jit(solution)/shard_map/while/body/eval_jaxpr/ppermute | solution.py:14
  472.3 7.8 all-to-all-done
  493.0 6.5 all-to-all-start.2
  508.7 17.5 %collective-permute-start = (bf16[8,128,256]{1,2,0:T(8,128)(2,1)}, bf16[8,128,256]{1,2,0:T(8,128)(2,1)S(1)}, u32[]{:S(2)}, u32[]{:S(2)}) collective-permute-start(bf16[8,128,256]{1,2,0:T(8,128)(2,1)} %get-tuple-element.525), channel_id=1, source_target_pairs={{8,0},{16,8},{24,16},{9,1},{17,9},{25,17},{10,2},{18,10},{26,18},{... | collective-permute-start | bytes 1572872 | tf_op jit(solution)/shard_map/while/body/eval_jaxpr/ppermute | solution.py:14
  583.2 12.2 %collective-permute-start = (bf16[8,128,256]{1,2,0:T(8,128)(2,1)}, bf16[8,128,256]{1,2,0:T(8,128)(2,1)S(1)}, u32[]{:S(2)}, u32[]{:S(2)}) collective-permute-start(bf16[8,128,256]{1,2,0:T(8,128)(2,1)} %get-tuple-element.525), channel_id=1, source_target_pairs={{8,0},{16,8},{24,16},{9,1},{17,9},{25,17},{10,2},{18,10},{26,18},{... | collective-permute-start | bytes 1572872 | tf_op jit(solution)/shard_map/while/body/eval_jaxpr/ppermute | solution.py:14
  621.9 7.8 all-to-all-done
  642.6 6.5 all-to-all-start.2
  658.3 17.5 %collective-permute-start = (bf16[8,128,256]{1,2,0:T(8,128)(2,1)}, bf16[8,128,256]{1,2,0:T(8,128)(2,1)S(1)}, u32[]{:S(2)}, u32[]{:S(2)}) collective-permute-start(bf16[8,128,256]{1,2,0:T(8,128)(2,1)} %get-tuple-element.525), channel_id=1, source_target_pairs={{8,0},{16,8},{24,16},{9,1},{17,9},{25,17},{10,2},{18,10},{26,18},{... | collective-permute-start | bytes 1572872 | tf_op jit(solution)/shard_map/while/body/eval_jaxpr/ppermute | solution.py:14
  732.7 12.2 %collective-permute-start = (bf16[8,128,256]{1,2,0:T(8,128)(2,1)}, bf16[8,128,256]{1,2,0:T(8,128)(2,1)S(1)}, u32[]{:S(2)}, u32[]{:S(2)}) collective-permute-start(bf16[8,128,256]{1,2,0:T(8,128)(2,1)} %get-tuple-element.525), channel_id=1, source_target_pairs={{8,0},{16,8},{24,16},{9,1},{17,9},{25,17},{10,2},{18,10},{26,18},{... | collective-permute-start | bytes 1572872 | tf_op jit(solution)/shard_map/while/body/eval_jaxpr/ppermute | solution.py:14
  771.5 7.8 all-to-all-done
  792.1 6.5 all-to-all-start.2
  807.9 17.5 %collective-permute-start = (bf16[8,128,256]{1,2,0:T(8,128)(2,1)}, bf16[8,128,256]{1,2,0:T(8,128)(2,1)S(1)}, u32[]{:S(2)}, u32[]{:S(2)}) collective-permute-start(bf16[8,128,256]{1,2,0:T(8,128)(2,1)} %get-tuple-element.525), channel_id=1, source_target_pairs={{8,0},{16,8},{24,16},{9,1},{17,9},{25,17},{10,2},{18,10},{26,18},{... | collective-permute-start | bytes 1572872 | tf_op jit(solution)/shard_map/while/body/eval_jaxpr/ppermute | solution.py:14
  (556 shorter events, 528.4 us)
Async XLA Ops:
  5.7 17.6 %all-to-all-start.1 = ((bf16[2,8,64,256]{3,0,1,2:T(2,128)(2,1)}), bf16[2,8,64,256]{3,0,1,2:T(2,128)(2,1)S(1)}, u32[]{:S(2)}, u32[]{:S(2)}) async-start(bf16[2,8,64,256]{3,0,1,2:T(2,128)(2,1)} %copy.163), calls=%async_computation.1 | async-start | bytes 1048576 | tf_op jit(solution)/shard_map/while/body/eval_jaxpr/all_to_all | solution.py:124
  23.3 18.3 %all-to-all-start = ((bf16[2,8,64,256]{3,0,1,2:T(2,128)(2,1)}), bf16[2,8,64,256]{3,0,1,2:T(2,128)(2,1)S(1)}, u32[]{:S(2)}, u32[]{:S(2)}) async-start(bf16[2,8,64,256]{3,0,1,2:T(2,128)(2,1)} %copy.162), calls=%async_computation | async-start | bytes 1048576 | tf_op jit(solution)/shard_map/while/body/eval_jaxpr/all_to_all | solution.py:136
  54.4 18.3 %all-to-all-start.2 = ((bf16[2,64,8,256]{3,2,0,1:T(8,128)(2,1)}), bf16[2,64,8,256]{3,2,0,1:T(8,128)(2,1)S(1)}, u32[]{:S(2)}, u32[]{:S(2)}) async-start(bf16[2,64,8,256]{3,2,0,1:T(8,128)(2,1)} %copy.164), calls=%async_computation.2 | async-start | bytes 1048576 | tf_op jit(solution)/shard_map/while/body/eval_jaxpr/all_to_all | solution.py:146
  81.6 14.0 %all-to-all-start.1 = ((bf16[2,8,64,256]{3,0,1,2:T(2,128)(2,1)}), bf16[2,8,64,256]{3,0,1,2:T(2,128)(2,1)S(1)}, u32[]{:S(2)}, u32[]{:S(2)}) async-start(bf16[2,8,64,256]{3,0,1,2:T(2,128)(2,1)} %copy.163), calls=%async_computation.1 | async-start | bytes 1048576 | tf_op jit(solution)/shard_map/while/body/eval_jaxpr/all_to_all | solution.py:124
  95.5 12.8 %all-to-all-start = ((bf16[2,8,64,256]{3,0,1,2:T(2,128)(2,1)}), bf16[2,8,64,256]{3,0,1,2:T(2,128)(2,1)S(1)}, u32[]{:S(2)}, u32[]{:S(2)}) async-start(bf16[2,8,64,256]{3,0,1,2:T(2,128)(2,1)} %copy.162), calls=%async_computation | async-start | bytes 1048576 | tf_op jit(solution)/shard_map/while/body/eval_jaxpr/all_to_all | solution.py:136
  121.2 12.6 %all-to-all-start.2 = ((bf16[2,64,8,256]{3,2,0,1:T(8,128)(2,1)}), bf16[2,64,8,256]{3,2,0,1:T(8,128)(2,1)S(1)}, u32[]{:S(2)}, u32[]{:S(2)}) async-start(bf16[2,64,8,256]{3,2,0,1:T(8,128)(2,1)} %copy.164), calls=%async_computation.2 | async-start | bytes 1048576 | tf_op jit(solution)/shard_map/while/body/eval_jaxpr/all_to_all | solution.py:146
  135.4 13.0 %collective-permute-start = (bf16[8,128,256]{1,2,0:T(8,128)(2,1)}, bf16[8,128,256]{1,2,0:T(8,128)(2,1)S(1)}, u32[]{:S(2)}, u32[]{:S(2)}) collective-permute-start(bf16[8,128,256]{1,2,0:T(8,128)(2,1)} %get-tuple-element.525), channel_id=1, source_target_pairs={{8,0},{16,8},{24,16},{9,1},{17,9},{25,17},{10,2},{18,10},{26,18},{... | collective-permute-start | bytes 1572872 | tf_op jit(solution)/shard_map/while/body/eval_jaxpr/ppermute | solution.py:14
  151.4 12.6 %all-to-all-start.1 = ((bf16[2,8,64,256]{3,0,1,2:T(2,128)(2,1)}), bf16[2,8,64,256]{3,0,1,2:T(2,128)(2,1)S(1)}, u32[]{:S(2)}, u32[]{:S(2)}) async-start(bf16[2,8,64,256]{3,0,1,2:T(2,128)(2,1)} %copy.163), calls=%async_computation.1 | async-start | bytes 1048576 | tf_op jit(solution)/shard_map/while/body/eval_jaxpr/all_to_all | solution.py:124
  164.0 17.0 %all-to-all-start = ((bf16[2,8,64,256]{3,0,1,2:T(2,128)(2,1)}), bf16[2,8,64,256]{3,0,1,2:T(2,128)(2,1)S(1)}, u32[]{:S(2)}, u32[]{:S(2)}) async-start(bf16[2,8,64,256]{3,0,1,2:T(2,128)(2,1)} %copy.162), calls=%async_computation | async-start | bytes 1048576 | tf_op jit(solution)/shard_map/while/body/eval_jaxpr/all_to_all | solution.py:136
  193.8 14.2 %all-to-all-start.2 = ((bf16[2,64,8,256]{3,2,0,1:T(8,128)(2,1)}), bf16[2,64,8,256]{3,2,0,1:T(8,128)(2,1)S(1)}, u32[]{:S(2)}, u32[]{:S(2)}) async-start(bf16[2,64,8,256]{3,2,0,1:T(8,128)(2,1)} %copy.164), calls=%async_computation.2 | async-start | bytes 1048576 | tf_op jit(solution)/shard_map/while/body/eval_jaxpr/all_to_all | solution.py:146
  209.7 19.1 %collective-permute-start = (bf16[8,128,256]{1,2,0:T(8,128)(2,1)}, bf16[8,128,256]{1,2,0:T(8,128)(2,1)S(1)}, u32[]{:S(2)}, u32[]{:S(2)}) collective-permute-start(bf16[8,128,256]{1,2,0:T(8,128)(2,1)} %get-tuple-element.525), channel_id=1, source_target_pairs={{8,0},{16,8},{24,16},{9,1},{17,9},{25,17},{10,2},{18,10},{26,18},{... | collective-permute-start | bytes 1572872 | tf_op jit(solution)/shard_map/while/body/eval_jaxpr/ppermute | solution.py:14
  231.9 12.6 %all-to-all-start.1 = ((bf16[2,8,64,256]{3,0,1,2:T(2,128)(2,1)}), bf16[2,8,64,256]{3,0,1,2:T(2,128)(2,1)S(1)}, u32[]{:S(2)}, u32[]{:S(2)}) async-start(bf16[2,8,64,256]{3,0,1,2:T(2,128)(2,1)} %copy.163), calls=%async_computation.1 | async-start | bytes 1048576 | tf_op jit(solution)/shard_map/while/body/eval_jaxpr/all_to_all | solution.py:124
  284.0 14.0 %collective-permute-start = (bf16[8,128,256]{1,2,0:T(8,128)(2,1)}, bf16[8,128,256]{1,2,0:T(8,128)(2,1)S(1)}, u32[]{:S(2)}, u32[]{:S(2)}) collective-permute-start(bf16[8,128,256]{1,2,0:T(8,128)(2,1)} %get-tuple-element.525), channel_id=1, source_target_pairs={{8,0},{16,8},{24,16},{9,1},{17,9},{25,17},{10,2},{18,10},{26,18},{... | collective-permute-start | bytes 1572872 | tf_op jit(solution)/shard_map/while/body/eval_jaxpr/ppermute | solution.py:14
  301.0 12.6 %all-to-all-start.1 = ((bf16[2,8,64,256]{3,0,1,2:T(2,128)(2,1)}), bf16[2,8,64,256]{3,0,1,2:T(2,128)(2,1)S(1)}, u32[]{:S(2)}, u32[]{:S(2)}) async-start(bf16[2,8,64,256]{3,0,1,2:T(2,128)(2,1)} %copy.163), calls=%async_computation.1 | async-start | bytes 1048576 | tf_op jit(solution)/shard_map/while/body/eval_jaxpr/all_to_all | solution.py:124
  313.6 17.0 %all-to-all-start = ((bf16[2,8,64,256]{3,0,1,2:T(2,128)(2,1)}), bf16[2,8,64,256]{3,0,1,2:T(2,128)(2,1)S(1)}, u32[]{:S(2)}, u32[]{:S(2)}) async-start(bf16[2,8,64,256]{3,0,1,2:T(2,128)(2,1)} %copy.162), calls=%async_computation | async-start | bytes 1048576 | tf_op jit(solution)/shard_map/while/body/eval_jaxpr/all_to_all | solution.py:136
  343.4 14.1 %all-to-all-start.2 = ((bf16[2,64,8,256]{3,2,0,1:T(8,128)(2,1)}), bf16[2,64,8,256]{3,2,0,1:T(8,128)(2,1)S(1)}, u32[]{:S(2)}, u32[]{:S(2)}) async-start(bf16[2,64,8,256]{3,2,0,1:T(8,128)(2,1)} %copy.164), calls=%async_computation.2 | async-start | bytes 1048576 | tf_op jit(solution)/shard_map/while/body/eval_jaxpr/all_to_all | solution.py:146
  359.2 19.2 %collective-permute-start = (bf16[8,128,256]{1,2,0:T(8,128)(2,1)}, bf16[8,128,256]{1,2,0:T(8,128)(2,1)S(1)}, u32[]{:S(2)}, u32[]{:S(2)}) collective-permute-start(bf16[8,128,256]{1,2,0:T(8,128)(2,1)} %get-tuple-element.525), channel_id=1, source_target_pairs={{8,0},{16,8},{24,16},{9,1},{17,9},{25,17},{10,2},{18,10},{26,18},{... | collective-permute-start | bytes 1572872 | tf_op jit(solution)/shard_map/while/body/eval_jaxpr/ppermute | solution.py:14
  381.4 12.6 %all-to-all-start.1 = ((bf16[2,8,64,256]{3,0,1,2:T(2,128)(2,1)}), bf16[2,8,64,256]{3,0,1,2:T(2,128)(2,1)S(1)}, u32[]{:S(2)}, u32[]{:S(2)}) async-start(bf16[2,8,64,256]{3,0,1,2:T(2,128)(2,1)} %copy.163), calls=%async_computation.1 | async-start | bytes 1048576 | tf_op jit(solution)/shard_map/while/body/eval_jaxpr/all_to_all | solution.py:124
  433.6 14.0 %collective-permute-start = (bf16[8,128,256]{1,2,0:T(8,128)(2,1)}, bf16[8,128,256]{1,2,0:T(8,128)(2,1)S(1)}, u32[]{:S(2)}, u32[]{:S(2)}) collective-permute-start(bf16[8,128,256]{1,2,0:T(8,128)(2,1)} %get-tuple-element.525), channel_id=1, source_target_pairs={{8,0},{16,8},{24,16},{9,1},{17,9},{25,17},{10,2},{18,10},{26,18},{... | collective-permute-start | bytes 1572872 | tf_op jit(solution)/shard_map/while/body/eval_jaxpr/ppermute | solution.py:14
  450.6 12.6 %all-to-all-start.1 = ((bf16[2,8,64,256]{3,0,1,2:T(2,128)(2,1)}), bf16[2,8,64,256]{3,0,1,2:T(2,128)(2,1)S(1)}, u32[]{:S(2)}, u32[]{:S(2)}) async-start(bf16[2,8,64,256]{3,0,1,2:T(2,128)(2,1)} %copy.163), calls=%async_computation.1 | async-start | bytes 1048576 | tf_op jit(solution)/shard_map/while/body/eval_jaxpr/all_to_all | solution.py:124
  463.2 17.0 %all-to-all-start = ((bf16[2,8,64,256]{3,0,1,2:T(2,128)(2,1)}), bf16[2,8,64,256]{3,0,1,2:T(2,128)(2,1)S(1)}, u32[]{:S(2)}, u32[]{:S(2)}) async-start(bf16[2,8,64,256]{3,0,1,2:T(2,128)(2,1)} %copy.162), calls=%async_computation | async-start | bytes 1048576 | tf_op jit(solution)/shard_map/while/body/eval_jaxpr/all_to_all | solution.py:136
  493.0 14.1 %all-to-all-start.2 = ((bf16[2,64,8,256]{3,2,0,1:T(8,128)(2,1)}), bf16[2,64,8,256]{3,2,0,1:T(8,128)(2,1)S(1)}, u32[]{:S(2)}, u32[]{:S(2)}) async-start(bf16[2,64,8,256]{3,2,0,1:T(8,128)(2,1)} %copy.164), calls=%async_computation.2 | async-start | bytes 1048576 | tf_op jit(solution)/shard_map/while/body/eval_jaxpr/all_to_all | solution.py:146
  508.7 19.2 %collective-permute-start = (bf16[8,128,256]{1,2,0:T(8,128)(2,1)}, bf16[8,128,256]{1,2,0:T(8,128)(2,1)S(1)}, u32[]{:S(2)}, u32[]{:S(2)}) collective-permute-start(bf16[8,128,256]{1,2,0:T(8,128)(2,1)} %get-tuple-element.525), channel_id=1, source_target_pairs={{8,0},{16,8},{24,16},{9,1},{17,9},{25,17},{10,2},{18,10},{26,18},{... | collective-permute-start | bytes 1572872 | tf_op jit(solution)/shard_map/while/body/eval_jaxpr/ppermute | solution.py:14
  531.0 12.6 %all-to-all-start.1 = ((bf16[2,8,64,256]{3,0,1,2:T(2,128)(2,1)}), bf16[2,8,64,256]{3,0,1,2:T(2,128)(2,1)S(1)}, u32[]{:S(2)}, u32[]{:S(2)}) async-start(bf16[2,8,64,256]{3,0,1,2:T(2,128)(2,1)} %copy.163), calls=%async_computation.1 | async-start | bytes 1048576 | tf_op jit(solution)/shard_map/while/body/eval_jaxpr/all_to_all | solution.py:124
  583.2 14.0 %collective-permute-start = (bf16[8,128,256]{1,2,0:T(8,128)(2,1)}, bf16[8,128,256]{1,2,0:T(8,128)(2,1)S(1)}, u32[]{:S(2)}, u32[]{:S(2)}) collective-permute-start(bf16[8,128,256]{1,2,0:T(8,128)(2,1)} %get-tuple-element.525), channel_id=1, source_target_pairs={{8,0},{16,8},{24,16},{9,1},{17,9},{25,17},{10,2},{18,10},{26,18},{... | collective-permute-start | bytes 1572872 | tf_op jit(solution)/shard_map/while/body/eval_jaxpr/ppermute | solution.py:14
  612.7 17.0 %all-to-all-start = ((bf16[2,8,64,256]{3,0,1,2:T(2,128)(2,1)}), bf16[2,8,64,256]{3,0,1,2:T(2,128)(2,1)S(1)}, u32[]{:S(2)}, u32[]{:S(2)}) async-start(bf16[2,8,64,256]{3,0,1,2:T(2,128)(2,1)} %copy.162), calls=%async_computation | async-start | bytes 1048576 | tf_op jit(solution)/shard_map/while/body/eval_jaxpr/all_to_all | solution.py:136
  642.6 14.1 %all-to-all-start.2 = ((bf16[2,64,8,256]{3,2,0,1:T(8,128)(2,1)}), bf16[2,64,8,256]{3,2,0,1:T(8,128)(2,1)S(1)}, u32[]{:S(2)}, u32[]{:S(2)}) async-start(bf16[2,64,8,256]{3,2,0,1:T(8,128)(2,1)} %copy.164), calls=%async_computation.2 | async-start | bytes 1048576 | tf_op jit(solution)/shard_map/while/body/eval_jaxpr/all_to_all | solution.py:146
  658.3 19.2 %collective-permute-start = (bf16[8,128,256]{1,2,0:T(8,128)(2,1)}, bf16[8,128,256]{1,2,0:T(8,128)(2,1)S(1)}, u32[]{:S(2)}, u32[]{:S(2)}) collective-permute-start(bf16[8,128,256]{1,2,0:T(8,128)(2,1)} %get-tuple-element.525), channel_id=1, source_target_pairs={{8,0},{16,8},{24,16},{9,1},{17,9},{25,17},{10,2},{18,10},{26,18},{... | collective-permute-start | bytes 1572872 | tf_op jit(solution)/shard_map/while/body/eval_jaxpr/ppermute | solution.py:14
  732.7 14.0 %collective-permute-start = (bf16[8,128,256]{1,2,0:T(8,128)(2,1)}, bf16[8,128,256]{1,2,0:T(8,128)(2,1)S(1)}, u32[]{:S(2)}, u32[]{:S(2)}) collective-permute-start(bf16[8,128,256]{1,2,0:T(8,128)(2,1)} %get-tuple-element.525), channel_id=1, source_target_pairs={{8,0},{16,8},{24,16},{9,1},{17,9},{25,17},{10,2},{18,10},{26,18},{... | collective-permute-start | bytes 1572872 | tf_op jit(solution)/shard_map/while/body/eval_jaxpr/ppermute | solution.py:14
  762.3 17.0 %all-to-all-start = ((bf16[2,8,64,256]{3,0,1,2:T(2,128)(2,1)}), bf16[2,8,64,256]{3,0,1,2:T(2,128)(2,1)S(1)}, u32[]{:S(2)}, u32[]{:S(2)}) async-start(bf16[2,8,64,256]{3,0,1,2:T(2,128)(2,1)} %copy.162), calls=%async_computation | async-start | bytes 1048576 | tf_op jit(solution)/shard_map/while/body/eval_jaxpr/all_to_all | solution.py:136
  792.1 14.1 %all-to-all-start.2 = ((bf16[2,64,8,256]{3,2,0,1:T(8,128)(2,1)}), bf16[2,64,8,256]{3,2,0,1:T(8,128)(2,1)S(1)}, u32[]{:S(2)}, u32[]{:S(2)}) async-start(bf16[2,64,8,256]{3,2,0,1:T(8,128)(2,1)} %copy.164), calls=%async_computation.2 | async-start | bytes 1048576 | tf_op jit(solution)/shard_map/while/body/eval_jaxpr/all_to_all | solution.py:146
  807.9 19.2 %collective-permute-start = (bf16[8,128,256]{1,2,0:T(8,128)(2,1)}, bf16[8,128,256]{1,2,0:T(8,128)(2,1)S(1)}, u32[]{:S(2)}, u32[]{:S(2)}) collective-permute-start(bf16[8,128,256]{1,2,0:T(8,128)(2,1)} %get-tuple-element.525), channel_id=1, source_target_pairs={{8,0},{16,8},{24,16},{9,1},{17,9},{25,17},{10,2},{18,10},{26,18},{... | collective-permute-start | bytes 1572872 | tf_op jit(solution)/shard_map/while/body/eval_jaxpr/ppermute | solution.py:14
  (45 other events, 194.4 us)
where the time goes:
time: 842 us; the launch traced here: 827 us
  starting transfers between devices  327 us (39%)
  matrix products  196 us (23%)
  waiting for transfers between devices  188 us (22%)
  local copies, waits for them, and re-layouts  104 us (12%)
    ppermute x11, starting transfers between devices, from_behind(): return lax.ppermute(block, axis, route)  150 us
    all_to_all x11, waiting for transfers between devices, advance(): lax.all_to_all(back_height, 'space', split_axis=1, concat_axis=2, tiled=T...  72.7 us
    dot_general x88, matrix products, adjoint(): return jnp.dot(operand, weights.T, preferred_element_type=jnp.float32)  67.4 us
    all_to_all x11, starting transfers between devices, advance(): lax.all_to_all(back_height, 'space', split_axis=1, concat_axis=2, tiled=T...  64 us
    all_to_all x11, waiting for transfers between devices, advance(): lax.all_to_all(row_spectrum(grad_in, w_table, True).astype(jnp.bfloat16),...  63.7 us
    all_to_all x11, starting transfers between devices, advance(): lax.all_to_all(row_spectrum(act_block, w_table, False), 'space', split_ax...  56.9 us
    all_to_all x11, starting transfers between devices, advance(): lax.all_to_all(row_spectrum(grad_in, w_table, True).astype(jnp.bfloat16),...  56.3 us
    all_to_all x11, waiting for transfers between devices, advance(): lax.all_to_all(row_spectrum(act_block, w_table, False), 'space', split_ax...  44.7 us
  transfers between devices with their start and end apart: 44, of which 44 were waited for; matrix products, arithmetic and copies ran while one was open for 14% of the time, Pallas kernels for 0%

commit v1 on v0

v1 whole, which is shorter than its diff:
```python
import functools
import math

import jax
import jax.numpy as jnp
import numpy as np
from jax import lax
from jax.experimental import pallas as pl
from jax.experimental.pallas import tpu as pltpu
from jax.sharding import PartitionSpec as P

MESH = pl.DeviceIdType.MESH
BF16 = jnp.bfloat16
F32 = jnp.float32


def dft_tables(height, width, modes, ranks):
    rows = height // ranks
    cols = modes // ranks
    w = np.arange(width)
    k = np.arange(modes)
    wave = 2.0 * math.pi * ((k[:, None] * w[None, :]) % width) / width
    pair = np.stack([np.cos(wave), -np.sin(wave)], axis=1)
    row = np.einsum("kiw,hg->kihgw", pair, np.eye(rows))
    row = row.reshape(modes * 2 * rows, rows * width)
    h = np.arange(height)
    turn = 2.0 * math.pi * ((h[:, None] * h[None, :]) % height) / height
    c = np.cos(turn)
    s = np.sin(turn)
    full = np.stack([np.stack([c, s], axis=1), np.stack([-s, c], axis=1)])
    full = full.reshape(2, height, 2, ranks, rows)
    col = np.einsum("okish,mn->omksnih", full, np.eye(cols))
    col = col.reshape(2 * cols * height, ranks * cols * 2 * rows)
    flip = np.zeros((height, height))
    flip[h, (-h) % height] = 1.0
    return [jnp.asarray(t, BF16) for t in (row, col, col.T, row.T, flip)]


def gelu_slope(t):
    return (
        0.5 * (1.0 + lax.erf(t * 0.7071067811865476))
        + t * jnp.exp(-0.5 * t * t) * 0.3989422804014327
    )


def mm(a, b):
    return jnp.dot(a, b, preferred_element_type=F32)


def mmt(a, b):
    return lax.dot_general(a, b, (((1,), (1,)), ((), ())), preferred_element_type=F32)


def flat(x):
    ranks, rows, lanes = x.shape
    if rows % 16:
        return x.astype(F32).reshape(ranks * rows, lanes).astype(BF16)
    return x.reshape(ranks * rows, lanes)


def kernel(
    sizes,
    act_ref, cot_ref, first_ref, second_ref, bias_ref,
    row_ref, col_ref, icol_ref, irow_ref, flip_ref,
    out_ref,
    send_buf, recv_buf, back_buf, csend_buf, crecv_buf, g_buf, e_buf,
    a_ssem, a_rsem, b_ssem, b_rsem, c_ssem, c_rsem, g_ssem, g_rsem, e_ssem, e_rsem,
):
    ranks, stages, blocks, lanes, height, width = sizes
    me = lax.axis_index("space")
    stage = lax.axis_index("pipe")
    own = blocks // stages
    first_own = (stages - 1 - stage) * own
    tokens = g_buf.shape[1] // 2
    chunk = send_buf.shape[2]
    row_scale = 1.0 / math.sqrt(width)
    col_scale = 1.0 / math.sqrt(height)

    def columns(b):
        return pl.ds(pl.multiple_of(b * lanes, lanes), lanes)

    barrier = pltpu.get_barrier_semaphore()

    def greet_space(k, carry):
        pl.semaphore_signal(
            barrier, inc=1, device_id={"space": lax.rem(me + k, ranks)}, device_id_type=MESH
        )
        return carry

    def greet_pipe(k, carry):
        pl.semaphore_signal(
            barrier, inc=1, device_id={"pipe": lax.rem(stage + k, stages)}, device_id_type=MESH
        )
        return carry

    lax.fori_loop(1, ranks, greet_space, 0)
    lax.fori_loop(1, stages, greet_pipe, 0)
    pl.semaphore_wait(barrier, ranks + stages - 2)

    def scatter(value, sbuf, rbuf, ssem, rsem):
        sbuf[...] = value.reshape(ranks, chunk, lanes).astype(BF16)
        rbuf[me] = sbuf[me]

        def push(k, carry):
            peer = lax.rem(me + k, ranks)
            pltpu.make_async_remote_copy(
                src_ref=sbuf.at[peer],
                dst_ref=rbuf.at[me],
                send_sem=ssem,
                recv_sem=rsem,
                device_id={"space": peer},
                device_id_type=MESH,
            ).start()
            return carry

        lax.fori_loop(1, ranks, push, 0)

    def wait_all(buf, sem):
        part = buf.at[pl.ds(0, ranks - 1)]
        pltpu.make_async_copy(part, part, sem).wait()

    def wait_one(buf, sem):
        pltpu.make_async_copy(buf, buf, sem).wait()

    @pl.when(stage == stages - 1)
    def _():
        e_buf[...] = jnp.zeros_like(e_buf)

    def send_cot(j, carry):
        value = mm(row_ref[...], cot_ref[:, columns(first_own + j)]) * row_scale
        scatter(value, csend_buf.at[j], crecv_buf.at[j], c_ssem.at[j], c_rsem.at[j])
        return carry

    lax.fori_loop(0, own, send_cot, 0)

    def send_act(b, carry):
        value = mm(row_ref[...], act_ref[:, columns(b)]) * row_scale
        scatter(value, send_buf.at[b], recv_buf.at[b], a_ssem.at[b], a_rsem.at[b])
        return carry

    lax.fori_loop(0, blocks, send_act, 0)

    def make_grad(j, carry):
        b = first_own + j
        wait_all(crecv_buf.at[j], c_rsem.at[j])
        value = mm(col_ref[...], flat(crecv_buf[j])) * col_scale
        token = lax.rem(lax.broadcasted_iota(jnp.int32, value.shape, 0), tokens)
        mean = jnp.logical_and(token < height, me == 0)
        g_buf[b] = jnp.where(mean, value, 2.0 * value).astype(BF16)

        def push(k, inner):
            pltpu.make_async_remote_copy(
                src_ref=g_buf.at[b],
                dst_ref=g_buf.at[b],
                send_sem=g_ssem.at[j, k],
                recv_sem=g_rsem.at[b],
                device_id={"pipe": lax.rem(stage + k, stages)},
                device_id_type=MESH,
            ).start()
            return inner

        lax.fori_loop(1, stages, push, 0)
        return carry

    lax.fori_loop(0, own, make_grad, 0)

    def chain(b, carry):
        wait_all(recv_buf.at[b], a_rsem.at[b])
        spectra = (mm(col_ref[...], flat(recv_buf[b])) * col_scale).astype(BF16)
        s_re, s_im = spectra[:tokens], spectra[tokens:]
        a_re, a_im = first_ref[0, b], first_ref[1, b]
        slope_re = gelu_slope(mm(s_re, a_re) - mm(s_im, a_im) + bias_ref[0, b])
        slope_im = gelu_slope(mm(s_re, a_im) + mm(s_im, a_re) + bias_ref[1, b])

        mine = jnp.logical_and(b >= first_own, b < first_own + own)

        @pl.when(jnp.logical_not(mine))
        def _():
            wait_one(g_buf.at[b], g_rsem.at[b])

        @pl.when(stage < stages - 1)
        def _():
            wait_one(e_buf.at[b], e_rsem.at[b])

        e_re = e_buf[b, :tokens]
        e_im = e_buf[b, tokens:]
        flip = flip_ref[...]
        top_re = e_re[:height].astype(F32)
        top_im = e_im[:height].astype(F32)
        even_re = 0.5 * (top_re + mm(flip, e_re[:height]))
        even_im = 0.5 * (top_im - mm(flip, e_im[:height]))
        top_re = jnp.where(me == 0, even_re, top_re)
        top_im = jnp.where(me == 0, even_im, top_im)
        if tokens > height:
            add_re = jnp.concatenate([top_re, e_re[height:].astype(F32)], axis=0)
            add_im = jnp.concatenate([top_im, e_im[height:].astype(F32)], axis=0)
        else:
            add_re, add_im = top_re, top_im
        g_re = (g_buf[b, :tokens].astype(F32) + add_re).astype(BF16)
        g_im = (g_buf[b, tokens:].astype(F32) + add_im).astype(BF16)
        b_re, b_im = second_ref[0, b], second_ref[1, b]
        q_re = ((mmt(g_re, b_re) + mmt(g_im, b_im)) * slope_re).astype(BF16)
        q_im = ((mmt(g_im, b_re) - mmt(g_re, b_im)) * slope_im).astype(BF16)
        new_re = mmt(q_re, a_re) + mmt(q_im, a_im) + e_re.astype(F32)
        new_im = mmt(q_im, a_re) - mmt(q_re, a_im) + e_im.astype(F32)
        e_buf[b, :tokens] = new_re.astype(BF16)
        e_buf[b, tokens:] = new_im.astype(BF16)

        @pl.when(stage > 0)
        def _():
            pltpu.make_async_remote_copy(
                src_ref=e_buf.at[b],
                dst_ref=e_buf.at[b],
                send_sem=e_ssem.at[b],
                recv_sem=e_rsem.at[b],
                device_id={"pipe": lax.rem(stage + stages - 1, stages)},
                device_id_type=MESH,
            ).start()

        value = mm(icol_ref[...], e_buf[b]) * col_scale
        wait_all(send_buf.at[b], a_ssem.at[b])
        scatter(value, send_buf.at[b], back_buf.at[b], b_ssem.at[b], b_rsem.at[b])
        return carry

    lax.fori_loop(0, blocks, chain, 0)

    def finish(b, carry):
        wait_all(back_buf.at[b], b_rsem.at[b])
        value = mm(irow_ref[...], flat(back_buf[b])) * row_scale
        out_ref[:, columns(b)] = (cot_ref[:, columns(b)].astype(F32) + value).astype(BF16)
        wait_all(send_buf.at[b], b_ssem.at[b])

        @pl.when(stage > 0)
        def _():
            wait_one(e_buf.at[b], e_ssem.at[b])

        return carry

    lax.fori_loop(0, blocks, finish, 0)

    def drain(j, carry):
        wait_all(csend_buf.at[j], c_ssem.at[j])

        def one(k, inner):
            wait_one(g_buf.at[first_own + j], g_ssem.at[j, k])
            return inner

        lax.fori_loop(1, stages, one, 0)
        return carry

    lax.fori_loop(0, own, drain, 0)


def body(tables, activations, cotangent, w_first, w_second, b_first):
    ranks = lax.axis_size("space")
    stages = lax.axis_size("pipe")
    _, rows, width, channels = activations.shape
    blocks, lanes = w_first.shape[2], w_first.shape[3]
    height = rows * ranks
    cols = width // 2 // ranks
    own = blocks // stages
    chunk = 2 * cols * rows
    tokens = height * cols
    sizes = (ranks, stages, blocks, lanes, height, width)
    vmem = pl.BlockSpec(memory_space=pltpu.VMEM)
    wire = (blocks, ranks, chunk, lanes)
    dma = pltpu.SemaphoreType.DMA
    out = pl.pallas_call(
        functools.partial(kernel, sizes),
        out_shape=jax.ShapeDtypeStruct((rows * width, channels), BF16),
        in_specs=[vmem] * 10,
        out_specs=vmem,
        scratch_shapes=[
            pltpu.VMEM(wire, BF16),
            pltpu.VMEM(wire, BF16),
            pltpu.VMEM(wire, BF16),
            pltpu.VMEM((own,) + wire[1:], BF16),
            pltpu.VMEM((own,) + wire[1:], BF16),
            pltpu.VMEM((blocks, 2 * tokens, lanes), BF16),
            pltpu.VMEM((blocks, 2 * tokens, lanes), BF16),
            dma((blocks,)),
            dma((blocks,)),
            dma((blocks,)),
            dma((blocks,)),
            dma((own,)),
            dma((own,)),
            dma((own, stages)),
            dma((blocks,)),
            dma((blocks,)),
            dma((blocks,)),
        ],
        compiler_params=pltpu.CompilerParams(
            collective_id=0, has_side_effects=True, vmem_limit_bytes=62 * 1024 * 1024
        ),
    )(
        activations.reshape(rows * width, channels),
        cotangent.reshape(rows * width, channels),
        w_first[0],
        w_second[0],
        b_first[0].reshape(2, blocks, 1, lanes),
        *tables,
    )
    return out.reshape(activations.shape)


def solution(mesh):
    ranks = mesh.shape["space"]

    def run(activations, cotangent, w_first, w_second, b_first):
        height, width = activations.shape[1], activations.shape[2]
        tables = dft_tables(height, width, width // 2, ranks)
        inner = jax.shard_map(
            body,
            mesh=mesh,
            in_specs=(
                [P()] * 5,
                P("pipe", "space", None, None),
                P("space", None, None),
                P("pipe", None, None, None, None),
                P("pipe", None, None, None, None),
                P("pipe", None, None),
            ),
            out_specs=P("pipe", "space", None, None),
            check_vma=False,
        )
        return inner(tables, activations, cotangent, w_first, w_second, b_first)

    return run
```

time: 842 us -> 225 us (0.27); the launches traced: 827 us -> 225 us
  starting transfers between devices: 327 us -> 0 us
  Pallas kernels: 0 us -> 219 us
  matrix products: 196 us -> 0 us
  waiting for transfers between devices: 188 us -> 0 us
  local copies, waits for them, and re-layouts: 104 us -> 6.14 us
    pallas_call x0 -> x1, Pallas kernels: none -> 219 us  [body(): pl.pallas_call(functools.partial(kernel, sizes), out_shape=jax.ShapeDtype...]
    dot_general x231 -> x0, matrix products: 196 us -> none  [the longest x88 67.4 us: adjoint(): return jnp.dot(operand, weights.T, preferred_element_type=jnp.float32)]
    all_to_all x33 -> x0, waiting for transfers between devices: 181 us -> none  [the longest x11 72.7 us: advance(): lax.all_to_all(back_height, 'space', split_axis=1, concat_axis=2, tiled=T...]
    all_to_all x33 -> x0, starting transfers between devices: 177 us -> none  [the longest x11 64 us: advance(): lax.all_to_all(back_height, 'space', split_axis=1, concat_axis=2, tiled=T...]
    ppermute x11 -> x0, starting transfers between devices: 150 us -> none  [from_behind(): return lax.ppermute(block, axis, route)]
    dynamic_slice x44 -> x0, local copies, waits for them, and re-layouts: 29.7 us -> none  [the longest x22 14.8 us: advance(): lax.dynamic_slice_in_dim(cotangent, offset, block_size, 2)]
    convert_element_type x22 -> x0, local copies, waits for them, and re-layouts: 29.6 us -> none  [the longest x11 14.9 us: advance(): row_spectrum(grad_in, w_table, True).astype(jnp.bfloat16)]
    dynamic_update_slice x22 -> x0, local copies, waits for them, and re-layouts: 11.5 us -> none  [advance(): lax.dynamic_update_slice_in_dim(result, jnp.where(active, fresh, previous...]
  transfers between devices with their start and end apart: 44 -> 0, of which waited for: 44 -> 0; matrix products, arithmetic and copies ran while one was open for 14% -> 0% of each run, Pallas kernels for 0% -> 0%
where the time goes in v1:
time: 225 us
  Pallas kernels  219 us (97%)
  local copies, waits for them, and re-layouts  6.14 us (3%)
    pallas_call x1, Pallas kernels, body(): pl.pallas_call(functools.partial(kernel, sizes), out_shape=jax.ShapeDtype...  219 us
    unnamed x1, local copies, waits for them, and re-layouts  4.79 us

profile of v1, /device:TPU:15, one launch (start us, length us, event | category | flops | bytes accessed | tf_op | source)
XLA Modules:
  0.0 224.8 jit_solution(5029812939213387624)
XLA Ops:
  0.0 1.4 reshape_squeeze.3.bias_ref
  1.4 218.7 %shard_map.100 = bf16[1024,2048]{1,0:T(8,128)(2,1)} custom-call(bf16[1024,2048]{1,0:T(8,128)(2,1)} %bitcast.6, bf16[1024,2048]{1,0:T(8,128)(2,1)} %bitcast.7, bf16[2,8,256,256]{3,2,1,0:T(8,128)(2,1)} %bitcast.8, bf16[2,8,256,256]{3,2,1,0:T(8,128)(2,1)} %bitcast.9, f32[2,8,1,256]{3,2,1,0:T(1,128)} %reshape_squeeze.3.bias_ref, ...), custom_call_target="tpu_custom_call" | custom-call | tf_op jit(solution)/shard_map/pallas_call | solution.py:268
  220.1 4.8 %copy.12 = bf16[1,8,128,2048]{3,2,1,0:T(8,128)(2,1)} copy(bf16[1,8,128,2048]{3,2,1,0:T(8,128)(2,1)} %bitcast.5) | data formatting | bytes 8388608

commit v2 on v1

--- a/solution.py
+++ b/solution.py
@@ -60,9 +60,11 @@
 
 def kernel(
     sizes,
-    act_ref, cot_ref, first_ref, second_ref, bias_ref,
-    row_ref, col_ref, icol_ref, irow_ref, flip_ref,
-    out_ref,
+    act_hbm, cot_hbm, first_hbm, second_hbm, bias_ref,
+    row_hbm, col_hbm, icol_hbm, irow_hbm, flip_ref,
+    out_hbm,
+    act_ref, cot_ref, first_ref, second_ref, row_ref, col_ref, icol_ref, irow_ref,
+    act_sem, cot_sem, load_sem, out_sem,
     send_buf, recv_buf, back_buf, csend_buf, crecv_buf, g_buf, e_buf,
     a_ssem, a_rsem, b_ssem, b_rsem, c_ssem, c_rsem, g_ssem, g_rsem, e_ssem, e_rsem,
 ):
@@ -79,6 +81,46 @@
     def columns(b):
         return pl.ds(pl.multiple_of(b * lanes, lanes), lanes)
 
+    loads = [
+        pltpu.make_async_copy(src, dst, load_sem.at[i])
+        for i, (src, dst) in enumerate(
+            [
+                (row_hbm, row_ref),
+                (col_hbm, col_ref),
+                (first_hbm, first_ref),
+                (second_hbm, second_ref),
+                (icol_hbm, icol_ref),
+                (irow_hbm, irow_ref),
+            ]
+        )
+    ]
+
+    def load_act(b):
+        part = columns(b)
+        return pltpu.make_async_copy(act_hbm.at[:, part], act_ref.at[:, part], act_sem.at[b])
+
+    def load_cot(b):
+        part = columns(b)
+        return pltpu.make_async_copy(cot_hbm.at[:, part], cot_ref.at[:, part], cot_sem.at[b])
+
+    def store_out(b):
+        part = columns(b)
+        return pltpu.make_async_copy(act_ref.at[:, part], out_hbm.at[:, part], out_sem.at[b])
+
+    def each(low, high, act):
+        def step(i, carry):
+            act(i)
+            return carry
+
+        lax.fori_loop(low, high, step, 0)
+
+    loads[0].start()
+    each(0, own, lambda j: load_cot(first_own + j).start())
+    each(0, blocks, lambda b: load_act(b).start())
+    for load in loads[1:]:
+        load.start()
+    each(own, blocks, lambda j: load_cot(lax.rem(first_own + j, blocks)).start())
+
     barrier = pltpu.get_barrier_semaphore()
 
     def greet_space(k, carry):
@@ -126,7 +168,10 @@
     def _():
         e_buf[...] = jnp.zeros_like(e_buf)
 
+    loads[0].wait()
+
     def send_cot(j, carry):
+        load_cot(first_own + j).wait()
         value = mm(row_ref[...], cot_ref[:, columns(first_own + j)]) * row_scale
         scatter(value, csend_buf.at[j], crecv_buf.at[j], c_ssem.at[j], c_rsem.at[j])
         return carry
@@ -134,11 +179,14 @@
     lax.fori_loop(0, own, send_cot, 0)
 
     def send_act(b, carry):
+        load_act(b).wait()
         value = mm(row_ref[...], act_ref[:, columns(b)]) * row_scale
         scatter(value, send_buf.at[b], recv_buf.at[b], a_ssem.at[b], a_rsem.at[b])
         return carry
 
     lax.fori_loop(0, blocks, send_act, 0)
+
+    loads[1].wait()
 
     def make_grad(j, carry):
         b = first_own + j
@@ -164,13 +212,16 @@
 
     lax.fori_loop(0, own, make_grad, 0)
 
+    for load in loads[2:5]:
+        load.wait()
+
     def chain(b, carry):
         wait_all(recv_buf.at[b], a_rsem.at[b])
         spectra = (mm(col_ref[...], flat(recv_buf[b])) * col_scale).astype(BF16)
         s_re, s_im = spectra[:tokens], spectra[tokens:]
         a_re, a_im = first_ref[0, b], first_ref[1, b]
-        slope_re = gelu_slope(mm(s_re, a_re) - mm(s_im, a_im) + bias_ref[0, b])
-        slope_im = gelu_slope(mm(s_re, a_im) + mm(s_im, a_re) + bias_ref[1, b])
+        slope_re = gelu_slope(mm(s_re, a_re) - mm(s_im, a_im) + bias_ref[0, 0:1, columns(b)])
+        slope_im = gelu_slope(mm(s_re, a_im) + mm(s_im, a_re) + bias_ref[0, 1:2, columns(b)])
 
         mine = jnp.logical_and(b >= first_own, b < first_own + own)
 
@@ -224,10 +275,14 @@
 
     lax.fori_loop(0, blocks, chain, 0)
 
+    loads[5].wait()
+    each(own, blocks, lambda j: load_cot(lax.rem(first_own + j, blocks)).wait())
+
     def finish(b, carry):
         wait_all(back_buf.at[b], b_rsem.at[b])
         value = mm(irow_ref[...], flat(back_buf[b])) * row_scale
-        out_ref[:, columns(b)] = (cot_ref[:, columns(b)].astype(F32) + value).astype(BF16)
+        act_ref[:, columns(b)] = (cot_ref[:, columns(b)].astype(F32) + value).astype(BF16)
+        store_out(b).start()
         wait_all(send_buf.at[b], b_ssem.at[b])
 
         @pl.when(stage > 0)
@@ -249,6 +304,7 @@
         return carry
 
     lax.fori_loop(0, own, drain, 0)
+    each(0, blocks, lambda b: store_out(b).wait())
 
 
 def body(tables, activations, cotangent, w_first, w_second, b_first):
@@ -263,14 +319,24 @@
     tokens = height * cols
     sizes = (ranks, stages, blocks, lanes, height, width)
     vmem = pl.BlockSpec(memory_space=pltpu.VMEM)
+    hbm = pl.BlockSpec(memory_space=pl.ANY)
     wire = (blocks, ranks, chunk, lanes)
     dma = pltpu.SemaphoreType.DMA
     out = pl.pallas_call(
         functools.partial(kernel, sizes),
         out_shape=jax.ShapeDtypeStruct((rows * width, channels), BF16),
-        in_specs=[vmem] * 10,
-        out_specs=vmem,
+        in_specs=[hbm] * 4 + [vmem] + [hbm] * 4 + [vmem],
+        out_specs=hbm,
         scratch_shapes=[
+            pltpu.VMEM((rows * width, channels), BF16),
+            pltpu.VMEM((rows * width, channels), BF16),
+            pltpu.VMEM(w_first.shape[1:], BF16),
+            pltpu.VMEM(w_second.shape[1:], BF16),
+            *[pltpu.VMEM(t.shape, BF16) for t in tables[:4]],
+            dma((blocks,)),
+            dma((blocks,)),
+            dma((6,)),
+            dma((blocks,)),
             pltpu.VMEM(wire, BF16),
             pltpu.VMEM(wire, BF16),
             pltpu.VMEM(wire, BF16),
@@ -297,7 +363,7 @@
         cotangent.reshape(rows * width, channels),
         w_first[0],
         w_second[0],
-        b_first[0].reshape(2, blocks, 1, lanes),
+        b_first,
         *tables,
     )
     return out.reshape(activations.shape)

time: 225 us -> 217 us (0.964)
  Pallas kernels: 219 us -> 212 us
    pallas_call x1, Pallas kernels: 219 us -> 212 us  [body(): pl.pallas_call(functools.partial(kernel, sizes), out_shape=jax.ShapeDtype...]
where the time goes in v2:
time: 217 us; the launch traced here: 216 us
  Pallas kernels  212 us (98%)
  local copies, waits for them, and re-layouts  4.79 us (2%)
    pallas_call x1, Pallas kernels, body(): pl.pallas_call(functools.partial(kernel, sizes), out_shape=jax.ShapeDtype...  212 us
    unnamed x1, local copies, waits for them, and re-layouts  4.79 us

profile of v2, /device:TPU:15, one launch (start us, length us, event | category | flops | bytes accessed | tf_op | source)
XLA Modules:
  0.0 216.4 jit_solution(15075807708804092818)
XLA Ops:
  0.0 211.6 %shard_map.100 = bf16[1024,2048]{1,0:T(8,128)(2,1)} custom-call(bf16[1024,2048]{1,0:T(8,128)(2,1)} %bitcast.6, bf16[1024,2048]{1,0:T(8,128)(2,1)} %bitcast.7, bf16[2,8,256,256]{3,2,1,0:T(8,128)(2,1)} %bitcast.8, bf16[2,8,256,256]{3,2,1,0:T(8,128)(2,1)} %bitcast.9, f32[1,2,2048]{2,1,0:T(2,128)} %bias_ref.1, bf16[1024,1024]{1,0:T(8,128)(2,1)} %constant.10.clone.row_hbm, ...), custom_call_target="tpu_custom_call" | custom-call | tf_op jit(solution)/shard_map/pallas_call | solution.py:325
  211.6 4.8 %copy.12 = bf16[1,8,128,2048]{3,2,1,0:T(8,128)(2,1)} copy(bf16[1,8,128,2048]{3,2,1,0:T(8,128)(2,1)} %bitcast.5) | data formatting | bytes 8388608

commit v3 on v2

--- a/solution.py
+++ b/solution.py
@@ -305,6 +305,10 @@
 
     lax.fori_loop(0, own, drain, 0)
     each(0, blocks, lambda b: store_out(b).wait())
+
+
+def hand_over(src_ref, dst_ref):
+    dst_ref[...] = src_ref[...]
 
 
 def body(tables, activations, cotangent, w_first, w_second, b_first):
@@ -366,6 +370,14 @@
         b_first,
         *tables,
     )
+    tile = pl.BlockSpec((rows * width // 8, channels), lambda i: (i, 0))
+    out = pl.pallas_call(
+        hand_over,
+        grid=(8,),
+        out_shape=jax.ShapeDtypeStruct(out.shape, out.dtype),
+        in_specs=[tile],
+        out_specs=tile,
+    )(out)
     return out.reshape(activations.shape)
 
 

time: 217 us -> 218 us (level)
  Pallas kernels: 212 us -> 218 us
  local copies, waits for them, and re-layouts: 4.79 us -> 0 us
    pallas_call x0 -> x1, Pallas kernels: none -> 6.59 us  [body(): pl.pallas_call(hand_over, grid=(8,), out_shape=jax.ShapeDtypeStruct(out.s...]
    unnamed x1 -> x0, local copies, waits for them, and re-layouts: 4.79 us -> none
where the time goes in v3:
time: 218 us
  Pallas kernels  218 us (100%)
    pallas_call x1, Pallas kernels, body(): pl.pallas_call(functools.partial(kernel, sizes), out_shape=jax.ShapeDtype...  212 us
    pallas_call x1, Pallas kernels, body(): pl.pallas_call(hand_over, grid=(8,), out_shape=jax.ShapeDtypeStruct(out.s...  6.59 us

profile of v3, /device:TPU:15, one launch (start us, length us, event | category | flops | bytes accessed | tf_op | source)
XLA Modules:
  0.0 218.2 jit_solution(11532902099485289901)
XLA Ops:
  0.0 211.6 %shard_map.100.src_ref = bf16[1024,2048]{1,0:T(8,128)(2,1)} custom-call(bf16[1024,2048]{1,0:T(8,128)(2,1)} %bitcast.5, bf16[1024,2048]{1,0:T(8,128)(2,1)} %bitcast.6, bf16[2,8,256,256]{3,2,1,0:T(8,128)(2,1)} %bitcast.7, bf16[2,8,256,256]{3,2,1,0:T(8,128)(2,1)} %bitcast.8, f32[1,2,2048]{2,1,0:T(2,128)} %bias_ref.1, ...), custom_call_target="tpu_custom_call" | custom-call | tf_op jit(solution)/shard_map/pallas_call | solution.py:329
  211.6 6.6 %shard_map.101 = bf16[1024,2048]{1,0:T(8,128)(2,1)} custom-call(bf16[1024,2048]{1,0:T(8,128)(2,1)} %shard_map.100.src_ref), custom_call_target="tpu_custom_call" | custom-call | tf_op jit(solution)/shard_map/pallas_call | solution.py:374
